TPU v7x, 256 devices: a whole 4x4x8 slice. The times are simulated.
256 devices in a mesh: tm: 8 (over z_lo, core), height: 32 (over x, y, z_hi).
Axes of the slice: x: 4, y: 4, z: 8 (z_hi: 2, z_lo: 4; z = z_hi * 4 + z_lo), core: 2. Of those that a mesh axis runs over, the one named last changes fastest.
Arguments:
- clean_latents: bfloat16 [32, 128, 16, 3072], P('tm', 'height'), may hold values from -6 to 6
- gaussian_noise: bfloat16 [32, 128, 16, 3072], P('tm', 'height'), may hold values from -6 to 6
- text_states: bfloat16 [256, 3072], replicated, may hold values from -6 to 6
- queries: bfloat16 [32, 128, 16, 1536], P('tm', 'height'), may hold values from -40 to 40
- key_states: bfloat16 [32, 128, 16, 1536], P('tm', 'height'), may hold values from -8 to 8
- cotangent: bfloat16 [32, 128, 16, 1536], P('tm', 'height'), may hold values from -240 to 240
- text_keys: bfloat16 [256, 1536], replicated, may hold values from -6 to 6
- window_radii: int32 [12, 3], replicated, may hold values from 0 to 1
- timestep: int32 [1], replicated, may hold values from 200 to 799
- sketch_seed: int32 [1], replicated, may hold values from 0 to 65535
- down_image: bfloat16 [3072, 16], replicated, may hold values from -0.109375 to 0.109375
- up_image: bfloat16 [16, 1536], replicated, may hold values from -1.5 to 1.5
- down_text: bfloat16 [3072, 16], replicated, may hold values from -0.109375 to 0.109375
- up_text: bfloat16 [16, 1536], replicated, may hold values from -1.5 to 1.5
Outputs:
- value_grad: bfloat16 [32, 128, 16, 1536], P('tm', 'height')
- grad_sketch: float32 [16384], replicated
All inputs are finite; a program needn't handle non-finite values.
Results may differ from a plain program's by a relative error of at most 0.0075.
Values may be sent and summed in bfloat16 or wider, within the bound.
A program may use at most 128 MiB of HBM per device.

v0:
```python
import jax
import jax.numpy as jnp
from jax import lax
from jax.sharding import PartitionSpec as P

SKETCH = 16384
TW = 8


def padded_2(block, sides, width):
    for axis, dim in sides:
        count = lax.axis_size(axis)
        forward = [(i, i + 1) for i in range(count - 1)]
        backward = [(target, source) for source, target in forward]
        low = lax.ppermute(
            lax.slice_in_dim(block, block.shape[dim] - width, None, axis=dim), axis, forward
        )
        high = lax.ppermute(lax.slice_in_dim(block, 0, width, axis=dim), axis, backward)
        block = jnp.concatenate([low, block, high], axis=dim)
    return block


def shifted(array, axis, by):
    size = lax.axis_size(axis)
    pairs = [(i, i + by) for i in range(size) if 0 <= i + by < size]
    return lax.ppermute(array, axis, pairs)


def tile_rows(block, width):
    frame_count, row_count, col_count = (block.shape[0], block.shape[1], block.shape[2])
    rest = block.shape[3:]
    col_tiles = col_count // width
    shaped = block.reshape((frame_count, row_count, col_tiles, width) + rest)
    order = (2, 0, 1, 3) + tuple(range(4, 4 + len(rest)))
    return jnp.transpose(shaped, order).reshape((col_tiles, frame_count * row_count * width) + rest)


def region_rows(padded, width):
    col_count = padded.shape[2] - 2 * width
    views = [
        tile_rows(padded[:, :, shift_col * width : shift_col * width + col_count], width)
        for shift_col in range(3)
    ]
    return jnp.concatenate(views, axis=1)


def window_mask(
    radius, frame_tile, row_tile, frame_tiles, row_tiles, col_tiles, frame_count, row_count, width
):
    region = 27 * frame_count * row_count * width
    position = jnp.arange(region, dtype=jnp.int32)
    col_step = position // (9 * frame_count * row_count * width) - 1
    frame_step = position // (3 * row_count * width) % (3 * frame_count) // frame_count - 1
    row_step = position // width % (3 * row_count) // row_count - 1
    inside = (
        (jnp.abs(frame_step) <= radius[0])
        & (jnp.abs(row_step) <= radius[1])
        & (jnp.abs(col_step) <= radius[2])
    )
    inside = inside & (frame_tile + frame_step >= 0) & (frame_tile + frame_step < frame_tiles)
    inside = inside & (row_tile + row_step >= 0) & (row_tile + row_step < row_tiles)
    col_index = jnp.arange(col_tiles, dtype=jnp.int32)[:, None]
    return (
        inside[None, :]
        & (col_index + col_step[None, :] >= 0)
        & (col_index + col_step[None, :] < col_tiles)
    )


def forward_head(query_head, key_region, text_head, cot_head, allowed, score_scale):
    image_scores = (
        jnp.einsum("cqd,cld->cql", query_head, key_region, preferred_element_type=jnp.float32)
        * score_scale
    )
    image_scores = jnp.where(allowed[:, None, :], image_scores, -jnp.inf)
    text_scores = (
        jnp.einsum("cqd,td->cqt", query_head, text_head, preferred_element_type=jnp.float32)
        * score_scale
    )
    row_max = jnp.maximum(jnp.max(image_scores, axis=-1), jnp.max(text_scores, axis=-1))
    total = jnp.sum(jnp.exp(image_scores - row_max[..., None]), axis=-1) + jnp.sum(
        jnp.exp(text_scores - row_max[..., None]), axis=-1
    )
    log_total = row_max + jnp.log(total)
    text_probs = jnp.exp(text_scores - log_total[..., None]).astype(jnp.bfloat16)
    text_part = jnp.einsum("cqt,cqd->td", text_probs, cot_head, preferred_element_type=jnp.float32)
    return (image_scores, log_total, text_part)


def place_back(spread, frame_count, row_count, width):
    col_tiles, head_width = (spread.shape[0], spread.shape[2])
    shaped = spread.reshape(col_tiles, 3, 3 * frame_count, 3 * row_count, width, head_width)
    placed = jnp.zeros((3 * frame_count, 3 * row_count, col_tiles, width, head_width), jnp.float32)
    for shift_col in range(3):
        moved = jnp.transpose(shaped[:, shift_col], (1, 2, 0, 3, 4))
        moved = jnp.pad(moved, ((0, 0), (0, 0), (1, 1), (0, 0), (0, 0)))
        placed = placed + moved[:, :, 2 - shift_col : 2 - shift_col + col_tiles]
    return placed.reshape(3 * frame_count, 3 * row_count, col_tiles * width, head_width)


def sketch_signs(seed_value, rows, width):
    row_part = jnp.arange(rows, dtype=jnp.int32)[:, None] * width
    position = row_part + jnp.arange(width, dtype=jnp.int32)[None, :]
    mixed_bits = position * 1103515245 + seed_value * 12345 + 1013904223
    mixed_bits = mixed_bits ^ mixed_bits >> 16
    mixed_bits = mixed_bits * 73244475
    mixed_bits = mixed_bits ^ mixed_bits >> 16
    return (1 - 2 * (mixed_bits >> 7 & 1)).astype(jnp.float32)


def count_sketch(pieces, seed_value, width, sketch_scale):
    flat = jnp.concatenate([piece.reshape(-1) for piece in pieces]).reshape(-1, width)
    signed = flat * sketch_signs(seed_value, flat.shape[0], width)
    return jnp.sum(signed, axis=0) * sketch_scale


def text_grads(text_hidden, text_value, text_states, up_text):
    highest = lax.Precision.HIGHEST
    text_up_grad = jnp.dot(text_hidden.T, text_value, precision=highest)
    text_back = jnp.dot(text_value, up_text.astype(jnp.float32).T, precision=highest)
    text_down_grad = jnp.dot(text_states.astype(jnp.float32).T, text_back, precision=highest)
    return (text_down_grad, text_up_grad)


def per_device(
    clean_latents,
    gaussian_noise,
    text_states,
    queries,
    key_states,
    cotangent,
    text_keys,
    window_radii,
    timestep,
    sketch_seed,
    down_image,
    up_image,
    down_text,
    up_text,
):
    frame_count, row_count, col_count, value_width = queries.shape
    head_count = window_radii.shape[0]
    head_width = value_width // head_count
    col_tiles = col_count // TW
    score_scale = head_width ** (-0.5)
    frame_tile = lax.axis_index("tm")
    row_tile = lax.axis_index("height")
    frame_tiles = lax.axis_size("tm")
    row_tiles = lax.axis_size("height")
    pad_spec = ((0, 0), (0, 0), (TW, TW), (0, 0))
    key_pad = jnp.pad(padded_2(key_states, (("tm", 0), ("height", 1)), frame_count), pad_spec)
    own_q = tile_rows(queries, TW)
    own_c = tile_rows(cotangent, TW)
    head_ids = jnp.arange(head_count, dtype=jnp.int32)

    def head_mask(head_index):
        return window_mask(
            window_radii[head_index],
            frame_tile,
            row_tile,
            frame_tiles,
            row_tiles,
            col_tiles,
            frame_count,
            row_count,
            TW,
        )

    def forward(head_index):
        offset = head_index * head_width
        allowed = head_mask(head_index)
        query_head = lax.dynamic_slice_in_dim(own_q, offset, head_width, 2)
        cot_head = lax.dynamic_slice_in_dim(own_c, offset, head_width, 2)
        key_region = region_rows(lax.dynamic_slice_in_dim(key_pad, offset, head_width, 3), TW)
        text_head = lax.dynamic_slice_in_dim(text_keys, offset, head_width, 1)
        image_scores, log_total, text_part = forward_head(
            query_head, key_region, text_head, cot_head, allowed, score_scale
        )
        image_probs = jnp.exp(image_scores - log_total[..., None]).astype(jnp.bfloat16)
        spread = jnp.einsum(
            "cql,cqd->cld", image_probs, cot_head, preferred_element_type=jnp.float32
        )
        return (text_part, place_back(spread, frame_count, row_count, TW))

    text_part, head_out = lax.map(forward, head_ids)
    text_value = jnp.transpose(text_part, (1, 0, 2)).reshape(-1, value_width)
    middle = head_out[:, :, row_count : 2 * row_count]
    for direction, border in (
        (-1, head_out[:, :, :row_count]),
        (1, head_out[:, :, 2 * row_count :]),
    ):
        middle = middle + shifted(border.astype(jnp.bfloat16), "height", direction).astype(
            border.dtype
        )
    own_part = middle[:, frame_count : 2 * frame_count]
    for direction, border in ((-1, middle[:, :frame_count]), (1, middle[:, 2 * frame_count :])):
        own_part = own_part + shifted(border.astype(jnp.bfloat16), "tm", direction).astype(
            border.dtype
        )
    value_f32 = jnp.transpose(own_part, (1, 2, 3, 0, 4)).reshape(
        frame_count, row_count, col_count, value_width
    )
    value_grad = value_f32.astype(jnp.bfloat16)
    noise_level = timestep[0].astype(jnp.float32) / 1000.0
    mixed = (
        (1.0 - noise_level) * clean_latents.astype(jnp.float32)
        + noise_level * gaussian_noise.astype(jnp.float32)
    ).astype(jnp.bfloat16)
    mixed = mixed.reshape(-1, mixed.shape[3])
    flat_value = value_grad.reshape(-1, value_width)
    hidden = jnp.dot(mixed, down_image, preferred_element_type=jnp.float32).astype(jnp.bfloat16)
    grad_up = lax.dot_general(
        hidden, flat_value, (((0,), (0,)), ((), ())), preferred_element_type=jnp.float32
    )
    backward_low = lax.dot_general(
        flat_value, up_image, (((1,), (1,)), ((), ())), preferred_element_type=jnp.float32
    ).astype(jnp.bfloat16)
    grad_down = lax.dot_general(
        mixed, backward_low, (((0,), (0,)), ((), ())), preferred_element_type=jnp.float32
    )
    text_hidden = jnp.dot(text_states, down_text, preferred_element_type=jnp.float32)
    token_total = frame_count * row_count * col_count * frame_tiles * row_tiles
    param_total = 2 * grad_down.size + 2 * grad_up.size
    sketch_scale = (token_total * (param_total // SKETCH)) ** (-0.5)
    text_down_grad, text_up_grad = text_grads(text_hidden, text_value, text_states, up_text)
    local_sketch = count_sketch(
        (grad_down, grad_up, text_down_grad, text_up_grad), sketch_seed[0], SKETCH, sketch_scale
    )
    grad_sketch = lax.psum(local_sketch, ("tm", "height"))
    return (value_grad, grad_sketch)


def solution(mesh):
    return jax.shard_map(
        per_device,
        mesh=mesh,
        in_specs=(
            P("tm", "height", None, None),
            P("tm", "height", None, None),
            P(),
            P("tm", "height", None, None),
            P("tm", "height", None, None),
            P("tm", "height", None, None),
            P(),
            P(),
            P(),
            P(),
            P(),
            P(),
            P(),
            P(),
        ),
        out_specs=(P("tm", "height", None, None), P()),
        check_vma=False,
    )
```

profile of v0, /device:TPU:1, one launch (start us, length us, event | category | flops | bytes accessed | tf_op | source)
XLA Modules:
  0.0 920.2 jit_solution(15900157499959258757)
XLA Ops:
  7.2 5.1 collective-permute-start
  12.3 1.9 collective-permute-start.1
  14.2 7.3 collective-permute-done
  22.5 2.1 constant_dynamic-update-slice_fusion.1
  28.1 12.5 %collective-permute-start.2 = (bf16[12,4,16,1536]{3,2,1,0:T(8,128)(2,1)}, bf16[12,4,16,1536]{3,2,1,0:T(8,128)(2,1)}, u32[]{:S(2)}, u32[]{:S(2)}) collective-permute-start(bf16[12,4,16,1536]{3,2,1,0:T(8,128)(2,1)} %constant_dynamic-update-slice_fusion), channel_id=1, source_target_pairs={{0,1},{1,2},{2,3},{3,4},{4,5},{5,6},{6,7},{7,8},{8,9},{9,10},{10,1... | collective-permute-start | bytes 7077896 | tf_op jit(solution)/shard_map/ppermute | solution.py:15
  40.7 2.1 copy.51
  42.8 97.1 %collective-permute-done.3 = bf16[12,4,16,1536]{3,2,1,0:T(8,128)(2,1)} collective-permute-done((bf16[12,4,16,1536]{3,2,1,0:T(8,128)(2,1)}, bf16[12,4,16,1536]{3,2,1,0:T(8,128)(2,1)}, u32[]{:S(2)}, u32[]{:S(2)}) %collective-permute-start.3) | collective-permute-done | bytes 2359328 | tf_op jit(solution)/shard_map/ppermute | solution.py:18
  139.9 9.7 %fusion.52 = bf16[12,12,32,1536]{3,2,1,0:T(8,128)(2,1)} fusion(bf16[12,4,16,1536]{3,2,1,0:T(8,128)(2,1)} %collective-permute-done.3, bf16[12,4,16,1536]{3,2,1,0:T(8,128)(2,1)} %constant_dynamic-update-slice_fusion, bf16[12,4,16,1536]{3,2,1,0:T(8,128)(2,1)} %collective-permute-done.2), kind=kLoop, calls=%fused_computation.99 | loop fusion | flops 84934656 | bytes 21233664 | tf_op jit(solution)/shard_map/concatenate | solution.py:19
  149.6 213.1 %while.15 = (s32[]{:T(128)}, f32[12,256,128]{1,2,0:T(8,128)}, f32[12,12,12,16,128]{4,3,2,1,0:T(8,128)}, s32[12]{0:T(128)S(1)}, bf16[2,128,1536]{2,1,0:T(8,128)(2...) while((s32[]{:T(128)}, f32[12,256,128]{1,2,0:T(8,128)}, ...), condition=%wide.region_5.6_spmd, body=%wide.region_0.5_spmd.sunk | while | flops 499376128 | bytes 40042176 | solution.py:185
  169.7 1.9 dynamic-slice_bitcast_fusion.4
  187.6 2.0 dynamic-slice_bitcast_fusion.4
  193.3 1.9 compare_and_fusion.4
  228.6 1.9 compare_and_fusion.4
  258.5 2.0 dynamic-slice_bitcast_fusion.4
  282.0 1.9 compare_and_fusion.4
  347.4 2.0 dynamic-slice_bitcast_fusion.4
  353.1 1.9 compare_and_fusion.4
  362.7 9.7 %convert.8 = bf16[12,12,12,16,128]{4,3,2,1,0:T(8,128)(2,1)} convert(f32[12,12,12,16,128]{4,3,2,1,0:T(8,128)} %get-tuple-element.191) | non-fusion elementwise | flops 3538944 | bytes 21233664 | tf_op jit(solution)/shard_map/convert.3
  372.4 6.3 fusion.75
  378.7 42.7 %collective-permute-start.5 = (bf16[12,12,4,16,128]{4,3,2,1,0:T(8,128)(2,1)}, bf16[12,12,4,16,128]{4,3,2,1,0:T(8,128)(2,1)}, u32[]{:S(2)}, u32[]{:S(2)}) collective-permute-start(bf16[12,12,4,16,128]{4,3,2,1,0:T(8,128)(2,1)} %get-tuple-element.230), channel_id=1, source_target_pairs={{0,1},{1,2},{2,3},{3,4},{4,5},{5,6},{6,7},{7,8},{8,9},{9,10},{10,1... | collective-permute-start | bytes 7077896 | tf_op jit(solution)/shard_map/ppermute | solution.py:26
  424.5 2.6 add_convert_fusion
  427.1 34.4 %collective-permute-done.5 = bf16[12,12,4,16,128]{4,3,2,1,0:T(8,128)(2,1)} collective-permute-done((bf16[12,12,4,16,128]{4,3,2,1,0:T(8,128)(2,1)}, bf16[12,12,4,16,128]{4,3,2,1,0:T(8,128)(2,1)}, u32[]{:S(2)}, u32[]{:S(2)}) %collective-permute-start.5) | collective-permute-done | bytes 2359328 | tf_op jit(solution)/shard_map/ppermute | solution.py:26
  461.5 108.8 %collective-permute-done.4 = bf16[12,12,4,16,128]{4,3,2,1,0:T(8,128)(2,1)} collective-permute-done((bf16[12,12,4,16,128]{4,3,2,1,0:T(8,128)(2,1)}, bf16[12,12,4,16,128]{4,3,2,1,0:T(8,128)(2,1)}, u32[]{:S(2)}, u32[]{:S(2)}) %collective-permute-start.4) | collective-permute-done | bytes 2359328 | tf_op jit(solution)/shard_map/ppermute | solution.py:26
  570.3 7.4 fusion.71
  579.3 61.7 %collective-permute-start.7 = (bf16[12,4,4,16,128]{4,3,2,1,0:T(8,128)(2,1)}, bf16[12,4,4,16,128]{4,3,2,1,0:T(8,128)(2,1)}, u32[]{:S(2)}, u32[]{:S(2)}) collective-permute-start(bf16[12,4,4,16,128]{4,3,2,1,0:T(8,128)(2,1)} %get-tuple-element.232), channel_id=1, source_target_pairs={{0,32},{32,64},{64,96},{96,128},{128,160},{160,192},{192,224},{1,3... | collective-permute-start | bytes 2359304 | tf_op jit(solution)/shard_map/ppermute | solution.py:26
  641.1 2.1 collective-permute-start.6
  644.6 2.0 fusion.77
  650.9 3.8 collective-permute-done.6
  654.7 2.2 fusion.54
  659.3 2.2 fusion.55
  662.2 3.7 fusion.56
  672.2 239.7 %all-reduce.5.cloned.1.call-done = f32[16384]{0:T(1024)} async-done(((f32[16384]{0:T(1024)}), f32[16384]{0:T(1024)}) %all-reduce.5.cloned.1.call-update) | async-done | bytes 65552 | tf_op jit(solution)/shard_map/psum | solution.py:229
  (328 shorter events, 190.9 us)
Async XLA Ops:
  7.2 416.8 %copy-start = (bf16[256,3072]{1,0:T(8,128)(2,1)S(1)}, bf16[256,3072]{1,0:T(8,128)(2,1)}, u32[]{:S(2)}) copy-start(bf16[256,3072]{1,0:T(8,128)(2,1)} %param.18) | copy-start | bytes 4718596
  7.2 33.5 %copy-start.6 = (bf16[4,4,16,1536]{3,2,1,0:T(8,128)(2,1)S(1)}, bf16[4,4,16,1536]{3,2,1,0:T(8,128)(2,1)}, u32[]{:S(2)}) copy-start(bf16[4,4,16,1536]{3,2,1,0:T(8,128)(2,1)} %param.19) | copy-start | bytes 2359300
  7.2 904.7 %all-reduce.5.cloned.1.call-start = ((), (), s32[]{:S(2)}) async-start(), calls=%async_computation | async-start | bytes 131072 | tf_op jit(solution)/shard_map/psum | solution.py:229
  7.2 14.3 %collective-permute-start = (bf16[4,4,16,1536]{3,2,1,0:T(8,128)(2,1)}, bf16[4,4,16,1536]{3,2,1,0:T(8,128)(2,1)S(1)}, u32[]{:S(2)}, u32[]{:S(2)}) collective-permute-start(bf16[4,4,16,1536]{3,2,1,0:T(8,128)(2,1)} %param.20), channel_id=1, source_target_pairs={{0,32},{32,64},{64,96},{96,128},{128,160},{160,192},{192,224},{1,3... | collective-permute-start | bytes 2359304 | tf_op jit(solution)/shard_map/ppermute | solution.py:15
  12.3 13.5 %collective-permute-start.1 = (bf16[4,4,16,1536]{3,2,1,0:T(8,128)(2,1)}, bf16[4,4,16,1536]{3,2,1,0:T(8,128)(2,1)S(1)}, u32[]{:S(2)}, u32[]{:S(2)}) collective-permute-start(bf16[4,4,16,1536]{3,2,1,0:T(8,128)(2,1)} %param.20), channel_id=1, source_target_pairs={{32,0},{64,32},{96,64},{128,96},{160,128},{192,160},{224,192},{33,... | collective-permute-start | bytes 2359304 | tf_op jit(solution)/shard_map/ppermute | solution.py:18
  26.8 113.1 %collective-permute-start.3 = (bf16[12,4,16,1536]{3,2,1,0:T(8,128)(2,1)}, bf16[12,4,16,1536]{3,2,1,0:T(8,128)(2,1)}, u32[]{:S(2)}, u32[]{:S(2)}) collective-permute-start(bf16[12,4,16,1536]{3,2,1,0:T(8,128)(2,1)} %constant_dynamic-update-slice_fusion), channel_id=1, source_target_pairs={{1,0},{2,1},{3,2},{4,3},{5,4},{6,5},{7,6},{8,7},{9,8},{10,9},{11,1... | collective-permute-start | bytes 7077896 | tf_op jit(solution)/shard_map/ppermute | solution.py:18
  28.1 111.8 %collective-permute-start.2 = (bf16[12,4,16,1536]{3,2,1,0:T(8,128)(2,1)}, bf16[12,4,16,1536]{3,2,1,0:T(8,128)(2,1)}, u32[]{:S(2)}, u32[]{:S(2)}) collective-permute-start(bf16[12,4,16,1536]{3,2,1,0:T(8,128)(2,1)} %constant_dynamic-update-slice_fusion), channel_id=1, source_target_pairs={{0,1},{1,2},{2,3},{3,4},{4,5},{5,6},{6,7},{7,8},{8,9},{9,10},{10,1... | collective-permute-start | bytes 7077896 | tf_op jit(solution)/shard_map/ppermute | solution.py:15
  42.8 106.8 %copy-start.9 = (s32[12,3]{0,1:T(4,128)S(1)}, s32[12,3]{0,1:T(4,128)}, u32[]{:S(2)}) copy-start(s32[12,3]{0,1:T(4,128)} %param.23) | copy-start | bytes 436
  149.6 4.3 copy-start.4
  167.3 4.4 copy-start.4
  183.8 1.2 copy-start.5
  185.1 4.5 copy-start.4
  202.9 4.3 copy-start.4
  220.6 4.3 copy-start.4
  238.3 4.3 copy-start.4
  256.1 4.5 copy-start.4
  272.7 1.2 copy-start.5
  273.9 4.3 copy-start.4
  291.6 4.3 copy-start.4
  309.3 4.4 copy-start.4
  325.9 1.3 copy-start.5
  327.1 4.4 copy-start.4
  344.9 4.4 copy-start.4
  372.4 51.6 %copy-start.8 = (bf16[3072,16]{0,1:T(8,128)(2,1)S(1)}, bf16[3072,16]{0,1:T(8,128)(2,1)}, u32[]{:S(2)}) copy-start(bf16[3072,16]{0,1:T(8,128)(2,1)} %param.28) | copy-start | bytes 294916
  378.7 82.8 %collective-permute-start.5 = (bf16[12,12,4,16,128]{4,3,2,1,0:T(8,128)(2,1)}, bf16[12,12,4,16,128]{4,3,2,1,0:T(8,128)(2,1)}, u32[]{:S(2)}, u32[]{:S(2)}) collective-permute-start(bf16[12,12,4,16,128]{4,3,2,1,0:T(8,128)(2,1)} %get-tuple-element.230), channel_id=1, source_target_pairs={{0,1},{1,2},{2,3},{3,4},{4,5},{5,6},{6,7},{7,8},{8,9},{9,10},{10,1... | collective-permute-start | bytes 7077896 | tf_op jit(solution)/shard_map/ppermute | solution.py:26
  421.4 148.9 %collective-permute-start.4 = (bf16[12,12,4,16,128]{4,3,2,1,0:T(8,128)(2,1)}, bf16[12,12,4,16,128]{4,3,2,1,0:T(8,128)(2,1)}, u32[]{:S(2)}, u32[]{:S(2)}) collective-permute-start(bf16[12,12,4,16,128]{4,3,2,1,0:T(8,128)(2,1)} %get-tuple-element.229), channel_id=1, source_target_pairs={{1,0},{2,1},{3,2},{4,3},{5,4},{6,5},{7,6},{8,7},{9,8},{10,9},{11,1... | collective-permute-start | bytes 7077896 | tf_op jit(solution)/shard_map/ppermute | solution.py:26
  577.7 65.5 %copy-start.3 = (f32[12,256,128]{1,2,0:T(8,128)S(1)}, f32[12,256,128]{1,2,0:T(8,128)}, u32[]{:S(2)}) copy-start(f32[12,256,128]{1,2,0:T(8,128)} %get-tuple-element.192) | copy-start | bytes 4718596
  577.7 66.9 %copy-start.10 = (bf16[16,1536]{1,0:T(8,128)(2,1)S(1)}, bf16[16,1536]{1,0:T(8,128)(2,1)}, u32[]{:S(2)}) copy-start(bf16[16,1536]{1,0:T(8,128)(2,1)} %param.29) | copy-start | bytes 147460
  579.3 71.6 %collective-permute-start.7 = (bf16[12,4,4,16,128]{4,3,2,1,0:T(8,128)(2,1)}, bf16[12,4,4,16,128]{4,3,2,1,0:T(8,128)(2,1)}, u32[]{:S(2)}, u32[]{:S(2)}) collective-permute-start(bf16[12,4,4,16,128]{4,3,2,1,0:T(8,128)(2,1)} %get-tuple-element.232), channel_id=1, source_target_pairs={{0,32},{32,64},{64,96},{96,128},{128,160},{160,192},{192,224},{1,3... | collective-permute-start | bytes 2359304 | tf_op jit(solution)/shard_map/ppermute | solution.py:26
  641.1 13.6 %collective-permute-start.6 = (bf16[12,4,4,16,128]{4,3,2,1,0:T(8,128)(2,1)}, bf16[12,4,4,16,128]{4,3,2,1,0:T(8,128)(2,1)}, u32[]{:S(2)}, u32[]{:S(2)}) collective-permute-start(bf16[12,4,4,16,128]{4,3,2,1,0:T(8,128)(2,1)} %get-tuple-element.231), channel_id=1, source_target_pairs={{32,0},{64,32},{96,64},{128,96},{160,128},{192,160},{224,192},{33,... | collective-permute-start | bytes 2359304 | tf_op jit(solution)/shard_map/ppermute | solution.py:26
  662.2 5.5 copy-start.7
  667.7 3.5 copy-start.2
  (10 other events, 11.9 us)
Sparse Core Ops, SparseCore 0:
  671.3 240.5 all-reduce.4
where the time goes:
time: 925 us; the launch traced here: 920 us
  waiting for transfers between devices  492 us (53%)
  starting transfers between devices  129 us (14%)
  matrix products  89.3 us (10%)
  other arithmetic  82 us (9%)
  local copies, waits for them, and re-layouts  81.4 us (9%)
  loops' own time  31 us (3%)
  between operations  15.5 us (2%)
    psum x1, waiting for transfers between devices, per_device(): grad_sketch = lax.psum(local_sketch, ('tm', 'height'))  240 us
    ppermute x4, waiting for transfers between devices, shifted(): return lax.ppermute(array, axis, pairs)  147 us
    ppermute x4, starting transfers between devices, shifted(): return lax.ppermute(array, axis, pairs)  108 us
    ppermute x2, waiting for transfers between devices, padded_2(): lax.ppermute(lax.slice_in_dim(block, 0, width, axis=dim), axis, backward)  98.3 us
    reshape x50, local copies, waits for them, and re-layouts, tile_rows(): shaped = block.reshape((frame_count, row_count, col_tiles, width) + rest)  38.7 us
    another operation x1, loops' own time, per_device(): text_part, head_out = lax.map(forward, head_ids)  31 us
    and x12, other arithmetic, window_mask(): inside & (row_tile + row_step >= 0) & (row_tile + row_step < row_tiles)  23 us
    dot_general x12, matrix products, forward(): jnp.einsum('cql,cqd->cld', image_probs, cot_head, preferred_element_type=...  22.2 us
  transfers between devices with their start and end apart: 9, of which 7 were waited for; matrix products, arithmetic and copies ran while one was open for 2% of the time, Pallas kernels for 0%

commit v1 on v0

--- a/solution.py
+++ b/solution.py
@@ -226,7 +226,8 @@
     local_sketch = count_sketch(
         (grad_down, grad_up, text_down_grad, text_up_grad), sketch_seed[0], SKETCH, sketch_scale
     )
-    grad_sketch = lax.psum(local_sketch, ("tm", "height"))
+    shards = lax.all_gather(local_sketch, ("tm", "height"), axis=0, tiled=False)
+    grad_sketch = shards.sum(axis=0)
     return (value_grad, grad_sketch)
 
 

time: 925 us -> 1450 us (1.57)
  waiting for transfers between devices: 492 us -> 986 us
  local copies, waits for them, and re-layouts: 81.4 us -> 98.1 us
    all_gather x0 -> x1, waiting for transfers between devices: none -> 733 us  [per_device(): shards = lax.all_gather(local_sketch, ('tm', 'height'), axis=0, tiled=False)]
    psum x1 -> x0, waiting for transfers between devices: 240 us -> none  [per_device(): grad_sketch = lax.psum(local_sketch, ('tm', 'height'))]
    all_gather x0 -> x1, local copies, waits for them, and re-layouts: none -> 18.2 us  [per_device(): shards = lax.all_gather(local_sketch, ('tm', 'height'), axis=0, tiled=False)]
  transfers between devices with their start and end apart: 9 -> 9, of which waited for: 7 -> 7; matrix products, arithmetic and copies ran while one was open for 2% -> 1% of each run, Pallas kernels for 0% -> 0%
where the time goes in v1:
time: 1450 us; the launch traced here: 1440 us
  waiting for transfers between devices  986 us (68%)
  starting transfers between devices  129 us (9%)
  local copies, waits for them, and re-layouts  98.1 us (7%)
  matrix products  89.3 us (6%)
  other arithmetic  89.2 us (6%)
  loops' own time  31 us (2%)
  between operations  15.5 us (1%)
    all_gather x1, waiting for transfers between devices, per_device(): shards = lax.all_gather(local_sketch, ('tm', 'height'), axis=0, tiled=False)  733 us
    ppermute x4, waiting for transfers between devices, shifted(): return lax.ppermute(array, axis, pairs)  147 us
    ppermute x4, starting transfers between devices, shifted(): return lax.ppermute(array, axis, pairs)  108 us
    ppermute x2, waiting for transfers between devices, padded_2(): lax.ppermute(lax.slice_in_dim(block, 0, width, axis=dim), axis, backward)  98.3 us
    reshape x50, local copies, waits for them, and re-layouts, tile_rows(): shaped = block.reshape((frame_count, row_count, col_tiles, width) + rest)  38.7 us
    another operation x1, loops' own time, per_device(): text_part, head_out = lax.map(forward, head_ids)  31 us
  transfers between devices with their start and end apart: 9, of which 7 were waited for; matrix products, arithmetic and copies ran while one was open for 1% of the time, Pallas kernels for 0%

profile of v1, /device:TPU:1, one launch (start us, length us, event | category | flops | bytes accessed | tf_op | source)
XLA Modules:
  0.0 1437.4 jit_solution(6029774690953000315)
XLA Ops:
  7.2 5.1 collective-permute-start
  12.3 1.9 collective-permute-start.1
  14.2 7.3 collective-permute-done
  22.5 2.1 constant_dynamic-update-slice_fusion.1
  28.1 12.5 collective-permute-start.2
  40.7 2.1 copy.66
  42.8 97.1 %collective-permute-done.3 = bf16[12,4,16,1536]{3,2,1,0:T(8,128)(2,1)} collective-permute-done((bf16[12,4,16,1536]{3,2,1,0:T(8,128)(2,1)}, bf16[12,4,16,1536]{3,2,1,0:T(8,128)(2,1)}, u32[]{:S(2)}, u32[]{:S(2)}) %collective-permute-start.3) | collective-permute-done | bytes 2359328 | tf_op jit(solution)/shard_map/ppermute | solution.py:18
  139.9 9.7 fusion.52
  149.6 213.1 %while.15 = (s32[]{:T(128)}, f32[12,256,128]{1,2,0:T(8,128)}, f32[12,12,12,16,128]{4,3,2,1,0:T(8,128)}, s32[12]{0:T(128)S(1)}, bf16[2,128,1536]{2,1,0:T(8,128)(2...) while((s32[]{:T(128)}, f32[12,256,128]{1,2,0:T(8,128)}, ...), condition=%wide.region_5.6_spmd, body=%wide.region_0.5_spmd.sunk | while | flops 499376128 | bytes 40042176 | solution.py:185
  169.7 1.9 dynamic-slice_bitcast_fusion.4
  187.6 2.0 dynamic-slice_bitcast_fusion.4
  193.3 1.9 compare_and_fusion.4
  228.6 1.9 compare_and_fusion.4
  258.5 2.0 dynamic-slice_bitcast_fusion.4
  347.4 2.0 dynamic-slice_bitcast_fusion.4
  362.7 9.7 convert.8
  372.4 6.3 fusion.75
  378.7 42.7 %collective-permute-start.5 = (bf16[12,12,4,16,128]{4,3,2,1,0:T(8,128)(2,1)}, bf16[12,12,4,16,128]{4,3,2,1,0:T(8,128)(2,1)}, u32[]{:S(2)}, u32[]{:S(2)}) collective-permute-start(bf16[12,12,4,16,128]{4,3,2,1,0:T(8,128)(2,1)} %get-tuple-element.230), channel_id=1, source_target_pairs={{0,1},{1,2},{2,3},{3,4},{4,5},{5,6},{6,7},{7,8},{8,9},{9,10},{10,1... | collective-permute-start | bytes 7077896 | tf_op jit(solution)/shard_map/ppermute | solution.py:26
  424.5 2.6 add_convert_fusion
  427.1 34.4 %collective-permute-done.5 = bf16[12,12,4,16,128]{4,3,2,1,0:T(8,128)(2,1)} collective-permute-done((bf16[12,12,4,16,128]{4,3,2,1,0:T(8,128)(2,1)}, bf16[12,12,4,16,128]{4,3,2,1,0:T(8,128)(2,1)}, u32[]{:S(2)}, u32[]{:S(2)}) %collective-permute-start.5) | collective-permute-done | bytes 2359328 | tf_op jit(solution)/shard_map/ppermute | solution.py:26
  461.5 108.8 %collective-permute-done.4 = bf16[12,12,4,16,128]{4,3,2,1,0:T(8,128)(2,1)} collective-permute-done((bf16[12,12,4,16,128]{4,3,2,1,0:T(8,128)(2,1)}, bf16[12,12,4,16,128]{4,3,2,1,0:T(8,128)(2,1)}, u32[]{:S(2)}, u32[]{:S(2)}) %collective-permute-start.4) | collective-permute-done | bytes 2359328 | tf_op jit(solution)/shard_map/ppermute | solution.py:26
  570.3 7.4 fusion.71
  579.3 61.7 %collective-permute-start.7 = (bf16[12,4,4,16,128]{4,3,2,1,0:T(8,128)(2,1)}, bf16[12,4,4,16,128]{4,3,2,1,0:T(8,128)(2,1)}, u32[]{:S(2)}, u32[]{:S(2)}) collective-permute-start(bf16[12,4,4,16,128]{4,3,2,1,0:T(8,128)(2,1)} %get-tuple-element.232), channel_id=1, source_target_pairs={{0,32},{32,64},{64,96},{96,128},{128,160},{160,192},{192,224},{1,3... | collective-permute-start | bytes 2359304 | tf_op jit(solution)/shard_map/ppermute | solution.py:26
  641.1 2.1 collective-permute-start.6
  644.6 2.0 fusion.77
  650.9 3.8 collective-permute-done.6
  654.7 2.2 fusion.54
  659.3 2.2 fusion.55
  662.2 3.7 fusion.56
  672.2 733.0 %all-gather.3.cloned.1.call-done = f32[4194304]{0:T(1024)} async-done(((f32[16384]{0:T(1024)}), f32[4194304]{0:T(1024)}) %all-gather.3.cloned.1.call-update) | async-done | bytes 16777232 | tf_op jit(solution)/shard_map/all_gather | solution.py:229
  1405.1 18.2 %reshape.281 = f32[256,16384]{1,0:T(8,128)} reshape(f32[4194304]{0:T(1024)} %all-gather.3.cloned.1.call-done) | data formatting | bytes 33554432 | tf_op jit(solution)/shard_map/all_gather | solution.py:229
  1423.3 7.2 reduce_sum.45
  (329 shorter events, 193.3 us)
Async XLA Ops:
  7.2 416.8 %copy-start = (bf16[256,3072]{1,0:T(8,128)(2,1)S(1)}, bf16[256,3072]{1,0:T(8,128)(2,1)}, u32[]{:S(2)}) copy-start(bf16[256,3072]{1,0:T(8,128)(2,1)} %param.18) | copy-start | bytes 4718596
  7.2 33.5 %copy-start.6 = (bf16[4,4,16,1536]{3,2,1,0:T(8,128)(2,1)S(1)}, bf16[4,4,16,1536]{3,2,1,0:T(8,128)(2,1)}, u32[]{:S(2)}) copy-start(bf16[4,4,16,1536]{3,2,1,0:T(8,128)(2,1)} %param.19) | copy-start | bytes 2359300
  7.2 1397.9 %all-gather.3.cloned.1.call-start = ((), (), s32[]{:S(2)}) async-start(), calls=%async_computation | async-start | bytes 16842752 | tf_op jit(solution)/shard_map/all_gather | solution.py:229
  7.2 14.3 collective-permute-start
  12.3 13.5 collective-permute-start.1
  26.8 113.1 %collective-permute-start.3 = (bf16[12,4,16,1536]{3,2,1,0:T(8,128)(2,1)}, bf16[12,4,16,1536]{3,2,1,0:T(8,128)(2,1)}, u32[]{:S(2)}, u32[]{:S(2)}) collective-permute-start(bf16[12,4,16,1536]{3,2,1,0:T(8,128)(2,1)} %constant_dynamic-update-slice_fusion), channel_id=1, source_target_pairs={{1,0},{2,1},{3,2},{4,3},{5,4},{6,5},{7,6},{8,7},{9,8},{10,9},{11,1... | collective-permute-start | bytes 7077896 | tf_op jit(solution)/shard_map/ppermute | solution.py:18
  28.1 111.8 %collective-permute-start.2 = (bf16[12,4,16,1536]{3,2,1,0:T(8,128)(2,1)}, bf16[12,4,16,1536]{3,2,1,0:T(8,128)(2,1)}, u32[]{:S(2)}, u32[]{:S(2)}) collective-permute-start(bf16[12,4,16,1536]{3,2,1,0:T(8,128)(2,1)} %constant_dynamic-update-slice_fusion), channel_id=1, source_target_pairs={{0,1},{1,2},{2,3},{3,4},{4,5},{5,6},{6,7},{7,8},{8,9},{9,10},{10,1... | collective-permute-start | bytes 7077896 | tf_op jit(solution)/shard_map/ppermute | solution.py:15
  42.8 106.8 %copy-start.9 = (s32[12,3]{0,1:T(4,128)S(1)}, s32[12,3]{0,1:T(4,128)}, u32[]{:S(2)}) copy-start(s32[12,3]{0,1:T(4,128)} %param.23) | copy-start | bytes 436
  149.6 4.3 copy-start.4
  167.3 4.4 copy-start.4
  183.8 1.2 copy-start.5
  185.1 4.5 copy-start.4
  202.9 4.3 copy-start.4
  220.6 4.3 copy-start.4
  238.3 4.3 copy-start.4
  256.1 4.5 copy-start.4
  272.7 1.2 copy-start.5
  273.9 4.3 copy-start.4
  291.6 4.3 copy-start.4
  309.3 4.4 copy-start.4
  325.9 1.3 copy-start.5
  327.1 4.4 copy-start.4
  344.9 4.4 copy-start.4
  372.4 51.6 %copy-start.8 = (bf16[3072,16]{0,1:T(8,128)(2,1)S(1)}, bf16[3072,16]{0,1:T(8,128)(2,1)}, u32[]{:S(2)}) copy-start(bf16[3072,16]{0,1:T(8,128)(2,1)} %param.28) | copy-start | bytes 294916
  378.7 82.8 %collective-permute-start.5 = (bf16[12,12,4,16,128]{4,3,2,1,0:T(8,128)(2,1)}, bf16[12,12,4,16,128]{4,3,2,1,0:T(8,128)(2,1)}, u32[]{:S(2)}, u32[]{:S(2)}) collective-permute-start(bf16[12,12,4,16,128]{4,3,2,1,0:T(8,128)(2,1)} %get-tuple-element.230), channel_id=1, source_target_pairs={{0,1},{1,2},{2,3},{3,4},{4,5},{5,6},{6,7},{7,8},{8,9},{9,10},{10,1... | collective-permute-start | bytes 7077896 | tf_op jit(solution)/shard_map/ppermute | solution.py:26
  421.4 148.9 %collective-permute-start.4 = (bf16[12,12,4,16,128]{4,3,2,1,0:T(8,128)(2,1)}, bf16[12,12,4,16,128]{4,3,2,1,0:T(8,128)(2,1)}, u32[]{:S(2)}, u32[]{:S(2)}) collective-permute-start(bf16[12,12,4,16,128]{4,3,2,1,0:T(8,128)(2,1)} %get-tuple-element.229), channel_id=1, source_target_pairs={{1,0},{2,1},{3,2},{4,3},{5,4},{6,5},{7,6},{8,7},{9,8},{10,9},{11,1... | collective-permute-start | bytes 7077896 | tf_op jit(solution)/shard_map/ppermute | solution.py:26
  577.7 65.5 %copy-start.3 = (f32[12,256,128]{1,2,0:T(8,128)S(1)}, f32[12,256,128]{1,2,0:T(8,128)}, u32[]{:S(2)}) copy-start(f32[12,256,128]{1,2,0:T(8,128)} %get-tuple-element.192) | copy-start | bytes 4718596
  577.7 66.9 %copy-start.10 = (bf16[16,1536]{1,0:T(8,128)(2,1)S(1)}, bf16[16,1536]{1,0:T(8,128)(2,1)}, u32[]{:S(2)}) copy-start(bf16[16,1536]{1,0:T(8,128)(2,1)} %param.29) | copy-start | bytes 147460
  579.3 71.6 %collective-permute-start.7 = (bf16[12,4,4,16,128]{4,3,2,1,0:T(8,128)(2,1)}, bf16[12,4,4,16,128]{4,3,2,1,0:T(8,128)(2,1)}, u32[]{:S(2)}, u32[]{:S(2)}) collective-permute-start(bf16[12,4,4,16,128]{4,3,2,1,0:T(8,128)(2,1)} %get-tuple-element.232), channel_id=1, source_target_pairs={{0,32},{32,64},{64,96},{96,128},{128,160},{160,192},{192,224},{1,3... | collective-permute-start | bytes 2359304 | tf_op jit(solution)/shard_map/ppermute | solution.py:26
  641.1 13.6 collective-permute-start.6
  662.2 5.5 copy-start.7
  667.7 3.5 copy-start.2
  (10 other events, 11.9 us)
Sparse Core Ops, SparseCore 0:
  671.3 733.7 all-gather.2
